TPU v7x, 256 devices: a whole 4x4x8 slice. The times are simulated.
256 devices in a mesh: space: 16 (over y_lo, x, core), dp: 16 (over y_hi, z).
Axes of the slice: x: 4, y: 4 (y_hi: 2, y_lo: 2; y = y_hi * 2 + y_lo), z: 8, core: 2. Of those that a mesh axis runs over, the one named last changes fastest.
Arguments:
- deep_grad: bfloat16 [256, 64, 20, 512], P(('dp', 'space')), may hold values from -48 to 48
- deep_weight: bfloat16 [1024, 512], replicated, may hold values from -0.1875 to 0.1875
- pre_first: bfloat16 [256, 64, 20, 256], P('dp', 'space'), may hold values from -6 to 6
- relu_first: bfloat16 [256, 64, 20, 256], P('dp', 'space'), may hold values from 0 to 6
- pre_middle: bfloat16 [256, 64, 20, 256], P('dp', 'space'), may hold values from -6 to 6
- relu_middle: bfloat16 [256, 64, 20, 256], P('dp', 'space'), may hold values from 0 to 6
- pre_last: bfloat16 [256, 64, 20, 1024], P('dp', 'space'), may hold values from -6 to 6
- block_output: bfloat16 [256, 64, 20, 1024], P('dp', 'space'), may hold values from 0 to 6
- weight_middle: bfloat16 [2304, 256], replicated, may hold values from -0.125 to 0.125
- weight_last: bfloat16 [256, 1024], replicated, may hold values from -0.375 to 0.375
- norm_mean: float32 [1536], replicated, may hold values from -3 to 3
- norm_rstd: float32 [1536], replicated, may hold values from 0.5 to 2
- norm_gain: float32 [1536], replicated, may hold values from 0.1 to 1.9
Outputs:
- first_grad: bfloat16 [256, 64, 20, 256], P('dp', 'space')
- weight_grads: float32 [851968], P(('space', 'dp'))
- norm_grads: float32 [2, 1536], replicated
All inputs are finite; a program needn't handle non-finite values.
Results may differ from a plain program's by a relative error of at most 0.012.
Values may be sent and summed in bfloat16 or wider, within the bound.
A program may use at most 128 MiB of HBM per device.

v0:
```python
import math

import jax
import jax.numpy as jnp
from jax import lax
from jax.sharding import PartitionSpec as P


def extended(cells, sides, width):
    for axis, dim in sides:
        count = lax.axis_size(axis)
        ends = count - 1
        head = lax.slice_in_dim(cells, 0, width, axis=dim)
        tail = lax.slice_in_dim(cells, cells.shape[dim] - width, cells.shape[dim], axis=dim)
        cells = jnp.concatenate(
            [
                lax.ppermute(tail, axis, [(i, (i + 1) % count) for i in range(ends)]),
                cells,
                lax.ppermute(head, axis, [((i + 1) % count, i) for i in range(ends)]),
            ],
            axis=dim,
        )
    return cells


def norm_back(gradient, saved, centre, spread, gains, positions):
    normed = (saved.astype(jnp.float32) - centre) * spread
    totals = jnp.sum(gradient, axis=0)
    crossed = jnp.sum(gradient * normed, axis=0)
    group_totals, group_crossed = lax.psum((totals, crossed), "space")
    result = (
        gains * spread * (gradient - group_totals / positions - normed * group_crossed / positions)
    )
    return (result.astype(jnp.bfloat16), group_totals, group_crossed)


def tap_columns(padded):
    height = padded.shape[1] - 2
    breadth = padded.shape[2] - 2
    pieces = []
    for row_offset in (-1, 0, 1):
        for col_offset in (-1, 0, 1):
            pieces.append(
                padded[
                    :,
                    1 - row_offset : 1 - row_offset + height,
                    1 - col_offset : 1 - col_offset + breadth,
                    :,
                ]
            )
    stacked = jnp.concatenate(pieces, axis=-1)
    return stacked.reshape(-1, stacked.shape[-1])


def shards(
    deep_grad,
    deep_weight,
    pre_first,
    relu_first,
    pre_middle,
    relu_middle,
    pre_last,
    block_output,
    weight_middle,
    weight_last,
    norm_mean,
    norm_rstd,
    norm_gain,
):
    channels = block_output.shape[-1]
    inner = weight_middle.shape[1]
    group_size, slab_rows, breadth = (
        block_output.shape[0],
        block_output.shape[1],
        block_output.shape[2],
    )
    positions = float(group_size * slab_rows * breadth * lax.axis_size("space"))
    factor = 1.0 / math.sqrt(positions * lax.axis_size("dp"))
    grad_rows = deep_grad.reshape(-1, deep_grad.shape[-1])
    projected = jnp.dot(grad_rows, deep_weight.T, preferred_element_type=jnp.float32).astype(
        jnp.bfloat16
    )
    projected = projected.reshape(deep_grad.shape[:3] + (channels,))
    upstream = lax.all_to_all(projected, "space", split_axis=1, concat_axis=0, tiled=True)
    outer = jnp.where(
        block_output.reshape(-1, channels) > 0,
        upstream.reshape(-1, channels).astype(jnp.float32),
        0.0,
    )
    last_dz, last_totals, last_crossed = norm_back(
        outer,
        pre_last.reshape(-1, channels),
        norm_mean[2 * inner :],
        norm_rstd[2 * inner :],
        norm_gain[2 * inner :],
        positions,
    )
    middle_flat = relu_middle.reshape(-1, inner)
    middle_in = jnp.where(
        middle_flat > 0, jnp.dot(last_dz, weight_last.T, preferred_element_type=jnp.float32), 0.0
    )
    last_sum = jnp.dot(middle_flat.T, last_dz, preferred_element_type=jnp.float32)
    middle_dz, middle_totals, middle_crossed = norm_back(
        middle_in,
        pre_middle.reshape(-1, inner),
        norm_mean[inner : 2 * inner],
        norm_rstd[inner : 2 * inner],
        norm_gain[inner : 2 * inner],
        positions,
    )
    slab = middle_dz.reshape(group_size, slab_rows, breadth, inner)
    padded = extended(slab, (("space", 1),), 1)
    padded = jnp.pad(padded, ((0, 0), (0, 0), (1, 1), (0, 0)))
    columns = tap_columns(padded)
    middle_turned = (
        weight_middle.reshape(9, inner, inner).transpose(0, 2, 1).reshape(9 * inner, inner)
    )
    first_flat = relu_first.reshape(-1, inner)
    first_in = jnp.where(
        first_flat > 0, jnp.dot(columns, middle_turned, preferred_element_type=jnp.float32), 0.0
    )
    middle_sum = jnp.dot(first_flat.T, columns, preferred_element_type=jnp.float32)
    middle_sum = middle_sum.reshape(inner, 9, inner).transpose(1, 0, 2).reshape(9 * inner, inner)
    first_dz, first_totals, first_crossed = norm_back(
        first_in,
        pre_first.reshape(-1, inner),
        norm_mean[:inner],
        norm_rstd[:inner],
        norm_gain[:inner],
        positions,
    )
    first_grad = first_dz.reshape(relu_first.shape)
    flat_sums = jnp.concatenate([middle_sum.reshape(-1), last_sum.reshape(-1)]) * factor
    weight_grads = lax.psum_scatter(flat_sums, ("space", "dp"), scatter_dimension=0, tiled=True)
    moments = jnp.stack(
        [
            jnp.concatenate([first_crossed, middle_crossed, last_crossed]),
            jnp.concatenate([first_totals, middle_totals, last_totals]),
        ]
    )
    norm_grads = lax.psum(moments, "dp") * factor
    return (first_grad, weight_grads, norm_grads)


def solution(mesh):
    return jax.shard_map(
        shards,
        mesh=mesh,
        in_specs=(
            P(("dp", "space"), None, None, None),
            P(),
            P("dp", "space", None, None),
            P("dp", "space", None, None),
            P("dp", "space", None, None),
            P("dp", "space", None, None),
            P("dp", "space", None, None),
            P("dp", "space", None, None),
            P(),
            P(),
            P(),
            P(),
            P(),
        ),
        out_specs=(P("dp", "space", None, None), P(("space", "dp")), P()),
        check_vma=False,
    )
```

profile of v0, /device:TPU:1, one launch (start us, length us, event | category | flops | bytes accessed | tf_op | source)
XLA Modules:
  0.0 486.4 jit_solution(7083661934406735607)
XLA Ops:
  10.5 4.4 convolution_convert_fusion
  14.9 5.2 %reshape.119 = bf16[1,64,20,1024]{3,2,1,0:T(8,128)(2,1)} reshape(bf16[1280,1024]{1,0:T(8,128)(2,1)} %convolution_convert_fusion) | data formatting | bytes 5242880 | tf_op jit(solution)/shard_map/reshape | solution.py:83
  20.1 7.0 %all-to-all-start = ((bf16[1,64,20,1024]{3,2,0,1:T(8,128)(2,1)}), bf16[1,64,20,1024]{3,2,0,1:T(8,128)(2,1)S(1)}, u32[]{:S(2)}, u32[]{:S(2)}) async-start(bf16[1,64,20,1024]{3,2,0,1:T(8,128)(2,1)} %bitcast.34), calls=%async_computation | async-start | bytes 6291456 | tf_op jit(solution)/shard_map/all_to_all | solution.py:84
  37.5 2.5 reshape.130
  44.8 3.3 copy_convert_fusion
  48.1 5.7 %copy.84 = f32[16,4,20,1024]{3,2,1,0:T(8,128)} copy(f32[16,4,20,1024]{3,0,2,1:T(8,128)S(1)} %copy_convert_fusion) | data formatting | bytes 10485760 | tf_op jit(solution)/shard_map/convert_element_type | solution.py:27
  53.8 6.8 %reshape.128 = f32[1280,1024]{1,0:T(8,128)} reshape(f32[16,4,20,1024]{3,2,1,0:T(8,128)} %copy.84) | data formatting | bytes 10485760 | tf_op jit(solution)/shard_map/convert_element_type | solution.py:27
  60.6 8.3 %all-to-all-done = bf16[1,64,20,1024]{3,2,0,1:T(8,128)(2,1)S(1)} async-done(((bf16[1,64,20,1024]{3,2,0,1:T(8,128)(2,1)}), bf16[1,64,20,1024]{3,2,0,1:T(8,128)(2,1)S(1)}, u32[]{:S(2)}, u32[]{:S(2)}) %all-to-all-start) | async-done | bytes 2621472 | tf_op jit(solution)/shard_map/all_to_all | solution.py:84
  69.7 3.1 copy-done.2
  73.5 6.7 %fusion.2 = (f32[1024]{0:T(1024)S(1)}, f32[1024]{0:T(1024)S(1)}, pred[16,4,20,1024]{3,0,2,1:T(8,128)(4,1)}) fusion(f32[16,4,20,1024]{3,2,1,0:T(8,128)S(1)} %bitcast.32, f32[1024]{0:T(1024)S(1)} %get-tuple-element.51, f32[1024]{0:T(1024)S(1)} %slice.69, bf16[16,4,20,1024]{3,1,2,0:T(4,128)(2,1)S(1)} %copy-done.3, bf16[16,4,20,1024]{3,1,2,0:T(4,128)(2,1)S(1)} %copy-done.17), kind=kLoop, calls=%fused_computation.15 | loop fusion | flops 10483712 | bytes 11812864 | tf_op jit(solution)/shard_map/reduce_sum | solution.py:28
  80.2 37.9 %all-reduce.4 = (f32[1024]{0:T(1024)S(1)}, f32[1024]{0:T(1024)S(1)}) all-reduce(f32[1024]{0:T(1024)S(1)} %get-tuple-element.19, f32[1024]{0:T(1024)S(1)} %get-tuple-element.18), channel_id=1, replica_groups=mesh['space'=16,'dp'=16] {'space'}, use_global_device_ids=true, to_apply=%region_3.4 | all-reduce | flops 2048 | bytes 16384 | tf_op jit(solution)/shard_map/psum | solution.py:30
  118.1 3.8 copy.78
  121.9 3.8 gt.30
  125.7 2.9 reshape.126
  128.6 8.3 %fusion.17 = (f32[256]{0:T(256)S(1)}, f32[256]{0:T(256)S(1)}, f32[1280,256]{1,0:T(8,128)}) fusion(f32[256]{0:T(256)S(1)} %get-tuple-element.47, f32[1280,256]{1,0:T(8,128)} %reshape.129, f32[256]{0:T(256)S(1)} %get-tuple-element.49, pred[1280,256]{1,0:T(32,128)(4,1)S(1)} %copy-done.21, bf16[256,1024]{1,0:T(8,128)(2,1)} %param.22, ...), kind=kOutput, calls=%fused_computation.68 | convolution fusion | flops 684850688 | bytes 15294464 | tf_op jit(solution)/shard_map/dot_general | solution.py:100
  136.9 27.6 %all-reduce.3 = (f32[256]{0:T(256)S(1)}, f32[256]{0:T(256)S(1)}) all-reduce(f32[256]{0:T(256)S(1)} %get-tuple-element.23, f32[256]{0:T(256)S(1)} %get-tuple-element.22), channel_id=1, replica_groups=mesh['space'=16,'dp'=16] {'space'}, use_global_device_ids=true, to_apply=%region_7.8 | all-reduce | flops 512 | bytes 4096 | tf_op jit(solution)/shard_map/psum | solution.py:30
  170.6 12.0 %fusion.3 = f32[256,1024]{0,1:T(8,128)} fusion(f32[1024]{0:T(1024)S(1)} %get-tuple-element.28, f32[1024]{0:T(1024)S(1)} %broadcast_multiply_fusion.1, f32[1024]{0:T(1024)S(1)} %get-tuple-element.50, f32[1024]{0:T(1024)S(1)} %get-tuple-element.51, f32[1024]{0:T(1024)S(1)} %slice.69, bf16[16,4,20,1024]{3,1,2,0:T(4,128)(2,1)} %param.19, ...), kind=kOutput, calls=%fused_computation.16 | convolution fusion | flops 684195840 | bytes 10899456 | tf_op jit(solution)/shard_map/dot_general | solution.py:102
  189.3 2.9 copy-done.22
  196.3 2.7 constant_dynamic-update-slice_fusion.9
  198.9 6.5 %fusion.9 = f32[2304,256,1,1]{1,0,3,2:T(8,128)} fusion(bf16[16,4,20,2304]{3,2,1,0:T(8,128)(2,1)} %get-tuple-element.35, bf16[16,4,20,256]{3,1,2,0:T(4,128)(2,1)S(1)} %copy-done.19), kind=kOutput, calls=%fused_computation.30 | convolution fusion | flops 1509949440 | bytes 8912896 | tf_op jit(solution)/shard_map/dot_general | solution.py:122
  224.6 2.9 fusion.16
  227.5 25.9 %all-reduce.2 = (f32[256]{0:T(256)S(1)}, f32[256]{0:T(256)S(1)}) all-reduce(f32[256]{0:T(256)S(1)} %get-tuple-element.21, f32[256]{0:T(256)S(1)} %get-tuple-element.20), channel_id=1, replica_groups=mesh['space'=16,'dp'=16] {'space'}, use_global_device_ids=true, to_apply=%region_11.12 | all-reduce | flops 512 | bytes 4096 | tf_op jit(solution)/shard_map/psum | solution.py:30
  256.5 65.9 %psum.55 = f32[2,1536]{1,0:T(2,128)S(1)} all-reduce(f32[2,1536]{1,0:T(2,128)S(1)} %pad_maximum_fusion.2), channel_id=1, replica_groups=mesh['space'=16,'dp'=16] {'dp'}, use_global_device_ids=true, to_apply=%region_13.14 | all-reduce | flops 3072 | bytes 24576 | tf_op jit(solution)/shard_map/psum | solution.py:141
  323.0 154.9 %all-reduce.7.cloned.1.call-done = f32[851968]{0:T(1024)} async-done(((f32[851968]{0:T(1024)}), f32[851968]{0:T(1024)}) %all-reduce.7.cloned.1.call-update) | async-done | bytes 3407888
  (119 shorter events, 60.9 us)
Async XLA Ops:
  7.2 3.4 copy-start
  20.1 7.4 %copy-start.23 = (f32[1536]{0:T(1024)S(1)}, f32[1536]{0:T(1024)}, u32[]{:S(2)}) copy-start(f32[1536]{0:T(1024)} %param.23) | copy-start | bytes 18436
  20.1 48.9 %all-to-all-start = ((bf16[1,64,20,1024]{3,2,0,1:T(8,128)(2,1)}), bf16[1,64,20,1024]{3,2,0,1:T(8,128)(2,1)S(1)}, u32[]{:S(2)}, u32[]{:S(2)}) async-start(bf16[1,64,20,1024]{3,2,0,1:T(8,128)(2,1)} %bitcast.34), calls=%async_computation | async-start | bytes 6291456 | tf_op jit(solution)/shard_map/all_to_all | solution.py:84
  27.1 450.9 %all-reduce.7.cloned.1.call-start = ((), (), s32[]{:S(2)}) async-start(), calls=%async_computation.1 | async-start | bytes 6815744
  53.8 6.8 %copy-start.24 = (f32[1536]{0:T(1024)S(1)}, f32[1536]{0:T(1024)}, u32[]{:S(2)}) copy-start(f32[1536]{0:T(1024)} %param.25) | copy-start | bytes 18436
  53.8 6.8 %copy-start.25 = (f32[1536]{0:T(1024)S(1)}, f32[1536]{0:T(1024)}, u32[]{:S(2)}) copy-start(f32[1536]{0:T(1024)} %param.24) | copy-start | bytes 18436
  69.0 3.8 copy-start.3
  69.0 4.5 copy-start.17
  69.7 3.1 copy-start.2
  125.7 2.9 copy-start.21
  128.6 35.9 %copy-start.5 = (f32[1280,256]{1,0:T(8,128)S(1)}, f32[1280,256]{1,0:T(8,128)}, u32[]{:S(2)}) copy-start(f32[1280,256]{1,0:T(8,128)} %reshape.129) | copy-start | bytes 3932164
  166.3 19.1 %collective-permute-start = (bf16[16,1,20,256]{3,2,1,0:T(8,128)(2,1)S(1)}, bf16[16,1,20,256]{3,2,1,0:T(8,128)(2,1)S(1)}, u32[]{:S(2)}, u32[]{:S(2)}) collective-permute-start(bf16[16,1,20,256]{3,2,1,0:T(8,128)(2,1)S(1)} %get-tuple-element.42), channel_id=1, source_target_pairs={{0,16},{16,32},{32,48},{48,64},{64,80},{80,96},{96,112},{112,128},... | collective-permute-start | bytes 491528 | tf_op jit(solution)/shard_map/ppermute | solution.py:17
  168.2 17.2 %collective-permute-start.1 = (bf16[16,1,20,256]{3,2,1,0:T(8,128)(2,1)S(1)}, bf16[16,1,20,256]{3,2,1,0:T(8,128)(2,1)S(1)}, u32[]{:S(2)}, u32[]{:S(2)}) collective-permute-start(bf16[16,1,20,256]{3,2,1,0:T(8,128)(2,1)S(1)} %get-tuple-element.43), channel_id=1, source_target_pairs={{16,0},{32,16},{48,32},{64,48},{80,64},{96,80},{112,96},{128,112},... | collective-permute-start | bytes 491528 | tf_op jit(solution)/shard_map/ppermute | solution.py:19
  189.3 2.9 copy-start.22
  196.3 2.7 copy-start.19
  210.9 6.2 %copy-start.9 = (bf16[16,4,20,256]{3,2,1,0:T(8,128)(2,1)S(1)}, bf16[16,4,20,256]{3,2,1,0:T(8,128)(2,1)}, u32[]{:S(2)}) copy-start(bf16[16,4,20,256]{3,2,1,0:T(8,128)(2,1)} %get-tuple-element.39) | copy-start | bytes 1966084
  212.0 6.1 %copy-start.8 = (bf16[16,4,20,256]{3,2,1,0:T(8,128)(2,1)S(1)}, bf16[16,4,20,256]{3,2,1,0:T(8,128)(2,1)}, u32[]{:S(2)}) copy-start(bf16[16,4,20,256]{3,2,1,0:T(8,128)(2,1)} %get-tuple-element.40) | copy-start | bytes 1966084
  213.0 6.0 %copy-start.7 = (bf16[16,4,20,256]{3,2,1,0:T(8,128)(2,1)S(1)}, bf16[16,4,20,256]{3,2,1,0:T(8,128)(2,1)}, u32[]{:S(2)}) copy-start(bf16[16,4,20,256]{3,2,1,0:T(8,128)(2,1)} %get-tuple-element.41) | copy-start | bytes 1966084
  218.0 3.1 copy-start.12
  219.0 3.4 copy-start.16
  222.6 1.6 copy-start.4
  222.6 2.0 copy-start.18
  222.6 2.0 copy-start.20
  253.5 225.8 %copy-start.1 = (bf16[1024,512]{1,0:T(8,128)(2,1)S(1)}, bf16[1024,512]{1,0:T(8,128)(2,1)}, u32[]{:S(2)}) copy-start(bf16[1024,512]{1,0:T(8,128)(2,1)} %param.14) | copy-start | bytes 3145732
  (6 other events, 7.7 us)
Sparse Core Ops, SparseCore 0:
  211.0 266.8 all-reduce.6
where the time goes:
time: 491 us; the launch traced here: 486 us
  waiting for transfers between devices  163 us (33%)
  blocking collectives  157 us (32%)
  local copies, waits for them, and re-layouts  82.7 us (17%)
  matrix products  34.2 us (7%)
  other arithmetic  22.6 us (5%)
  between operations  14.7 us (3%)
  starting transfers between devices  11.7 us (2%)
    unnamed x2, waiting for transfers between devices  155 us
    psum x3, blocking collectives, norm_back(): group_totals, group_crossed = lax.psum((totals, crossed), 'space')  91.4 us
    psum x1, blocking collectives, shards(): norm_grads = lax.psum(moments, 'dp') * factor  65.9 us
    convert_element_type x6, local copies, waits for them, and re-layouts, norm_back(): normed = (saved.astype(jnp.float32) - centre) * spread  22.3 us
    unnamed x71, local copies, waits for them, and re-layouts  20.4 us
    concatenate x10, local copies, waits for them, and re-layouts, tap_columns(): stacked = jnp.concatenate(pieces, axis=-1)  14.8 us
    dot_general x1, matrix products, shards(): jnp.dot(middle_flat.T, last_dz, preferred_element_type=jnp.float32)  12 us
  transfers between devices with their start and end apart: 4, of which 2 were waited for; matrix products, arithmetic and copies ran while one was open for 13% of the time, Pallas kernels for 0%

commit v1 on v0

v1 whole, which is shorter than its diff:
```python
import functools
import math

import jax
import jax.numpy as jnp
from jax import lax
from jax.experimental import pallas as pl
from jax.experimental.pallas import tpu as pltpu
from jax.sharding import PartitionSpec as P

MESH = pl.DeviceIdType.MESH
F32 = jnp.float32
BF16 = jnp.bfloat16

NS = 16
ND = 16
GROUP = 16
SLAB = 4
COLS = 20
ROWS = 64
CH = 1024
MID = 256
MID4 = 512
POS = GROUP * SLAB * COLS
PLANE = GROUP * COLS
BLOCK = SLAB * COLS
FLAT = 9 * MID + CH
SHARE = FLAT // NS
PIECE = SHARE // ND
M = float(GROUP * ROWS * COLS)
FACTOR = 1.0 / math.sqrt(M * ND)
NT = (((1,), (1,)), ((), ()))


def folded(values):
    return jnp.sum(values.reshape(-1, 8, values.shape[-1]), axis=0)


def lanes(ref, rows):
    return jnp.concatenate([ref[0, rows, :], ref[1, rows, :]], axis=1)


def kernel(
    dg_hbm, wd_hbm, pf_hbm, rf_hbm, pm_hbm, rm_hbm, pz_hbm, bo_hbm, wm_hbm, wl_hbm,
    mean_ref, rstd_ref, gain_ref,
    out_hbm, wg_ref, ng_ref,
    dgv, send, recv, wd, bo4, pz4, pf4, rf4, pm4, rm4, wl, wcat,
    glast, ldz, zcm, gmid, stage, hstage, buf, rfh, rft, rmt, zfh, gfirst, ob4,
    acc, st1, st2, st3, std,
    zsend, gsend, zhalo, ghalo, masks,
    pflat, part, ra, sb, rb, tc, sc, rc,
    lsem, dsem, osem,
    a2a_s, a2a_r, s1s, s1r, s2s, s2r, s3s, s3r, sds, sdr, hs, hr,
    as_, ar_, bs_, br_, cs_, cr_,
):
    me = lax.axis_index("space")
    dp = lax.axis_index("dp")

    dg_copies = [
        pltpu.make_async_copy(
            dg_hbm.at[:, pl.ds(16 * u, 16), :], dgv.at[:, pl.ds(16 * u, 16), :], dsem.at[u]
        )
        for u in range(4)
    ]
    for copy in dg_copies:
        copy.start()
    loads = []

    def load(src, dst):
        copy = pltpu.make_async_copy(src, dst, lsem.at[len(loads)])
        copy.start()
        loads.append(copy)
        return copy

    def load_tiles(src, dst, count):
        return [load(src.at[:, :, pl.ds(128 * j, 128)], dst.at[j]) for j in range(count)]

    barrier = pltpu.get_barrier_semaphore()

    def greet(k, carry):
        pl.semaphore_signal(
            barrier, inc=1, device_id=(lax.rem(me + k, NS), dp), device_id_type=MESH
        )
        pl.semaphore_signal(
            barrier, inc=1, device_id=(me, lax.rem(dp + k, ND)), device_id_type=MESH
        )
        return carry

    lax.fori_loop(1, NS, greet, 0)

    ld_pm = load_tiles(pm_hbm, pm4, 2)
    ld_rm = load_tiles(rm_hbm, rm4, 2)
    ld_wd = [load(wd_hbm, wd)]
    ld_bo = load_tiles(bo_hbm, bo4, 8)
    ld_pz = load_tiles(pz_hbm, pz4, 8)
    ld_rf = load_tiles(rf_hbm, rf4, 2)
    ld_pf = load_tiles(pf_hbm, pf4, 2)
    ld_wl = [load(wl_hbm, wl)]
    ld_wc = [
        load(wm_hbm.at[pl.ds(t * MID, MID)], wcat.at[t // 3, :, pl.ds((t % 3) * MID, MID)])
        for t in range(9)
    ]

    bo = bo4.reshape(8, POS, 128)
    pz = pz4.reshape(8, POS, 128)
    pf = pf4.reshape(2, POS, 128)
    rf = rf4.reshape(2, POS, 128)
    pm = pm4.reshape(2, POS, 128)
    rm = rm4.reshape(2, POS, 128)
    ob = ob4.reshape(2, POS, 128)

    def exchange(target, sender):
        return pltpu.make_async_remote_copy(
            src_ref=send.at[target],
            dst_ref=recv.at[pl.ds(pl.multiple_of(sender * BLOCK, BLOCK), BLOCK)],
            send_sem=a2a_s.at[target],
            recv_sem=a2a_r.at[sender],
            device_id=(target, dp),
            device_id_type=MESH,
        )

    for copy in dg_copies:
        copy.wait()
    my_group = lax.div(me, 4)

    def pack(step, carry):
        u = lax.rem(my_group + jnp.where(step == 0, 2, jnp.where(step == 1, 1, jnp.where(step == 2, 3, 0))), 4)
        x = dgv[:, pl.ds(pl.multiple_of(u * 16, 16), 16), :].astype(F32)
        low = lax.broadcasted_iota(jnp.int32, (10, 8, MID4), 1) < 4
        for half in range(2):
            y = x[:, 8 * half : 8 * half + 8, :].reshape(10, 2, 8, MID4)
            even, odd = y[:, 0], y[:, 1]
            first = jnp.where(low, even, pltpu.roll(odd, 4, 1))
            second = jnp.where(low, pltpu.roll(even, 4, 1), odd)
            send[u * 4 + 2 * half] = first.reshape(BLOCK, MID4).astype(BF16)
            send[u * 4 + 2 * half + 1] = second.reshape(BLOCK, MID4).astype(BF16)

        @pl.when(step == 0)
        def _():
            pl.semaphore_wait(barrier, NS + ND - 2)

        for q in range(4):
            target = u * 4 + q

            @pl.when(target != me)
            def _():
                exchange(target, me).start()

        return carry

    lax.fori_loop(0, 4, pack, 0)
    recv[pl.ds(pl.multiple_of(me * BLOCK, BLOCK), BLOCK), :] = send[me]

    mean = lambda lo, n: mean_ref[pl.ds(lo, n)].reshape(1, n)
    rstd = lambda lo, n: rstd_ref[pl.ds(lo, n)].reshape(1, n)
    gain = lambda lo, n: gain_ref[pl.ds(lo, n)].reshape(1, n)

    def halo(src, dst, sem, to_up):
        slot = 0 if to_up else 1
        target = lax.rem(me + (NS - 1 if to_up else 1), NS)
        return pltpu.make_async_remote_copy(
            src_ref=src.at[slot],
            dst_ref=dst.at[1 - slot],
            send_sem=hs.at[sem, slot],
            recv_sem=hr.at[sem, 1 - slot],
            device_id=(target, dp),
            device_id_type=MESH,
        )

    def send_halos(src, dst, sem):
        @pl.when(me > 0)
        def _():
            halo(src, dst, sem, True).start()

        @pl.when(me < NS - 1)
        def _():
            halo(src, dst, sem, False).start()

    def wait_halos(src, dst, sem):
        @pl.when(me > 0)
        def _():
            halo(src, dst, sem, True).wait_send()
            halo(src, dst, sem, False).wait_recv()

        @pl.when(me < NS - 1)
        def _():
            halo(src, dst, sem, False).wait_send()
            halo(src, dst, sem, True).wait_recv()

    for copy in ld_pm:
        copy.wait()
    for l in range(2):
        raw = pm[l].astype(F32)
        stage[l, pl.ds(8, POS), :] = raw
        zcm[l] = raw - mean(MID + 128 * l, 128)
    for slot, h in ((0, 0), (1, SLAB - 1)):
        for l in range(2):
            zsend[slot, :, l * 128 : l * 128 + 128] = stage[
                l, pl.ds(8 + h, PLANE, stride=SLAB), :
            ].astype(BF16)
    send_halos(zsend, zhalo, 0)

    for copy in ld_rm:
        copy.wait()
    for l in range(2):
        rmt[pl.ds(l * 128, 128), :] = rm[l].T

    row = lax.broadcasted_iota(jnp.int32, (PLANE, 128), 0)
    column = lax.rem(row, COLS)
    masks[0] = jnp.where(column == COLS - 1, 0.0, 1.0)
    masks[1] = jnp.where(column == 0, 0.0, 1.0)

    for copy in ld_rf:
        copy.wait()
    for l in range(2):
        stage[l, pl.ds(8, POS), :] = rf[l].astype(F32)
    for h in range(SLAB):
        for l in range(2):
            rfh[pl.ds(h * PLANE, PLANE), l * 128 : l * 128 + 128] = stage[
                l, pl.ds(8 + h, PLANE, stride=SLAB), :
            ].astype(BF16)
    for l in range(2):
        rft[pl.ds(l * 128, 128), :] = rfh[:, l * 128 : l * 128 + 128].T

    for copy in ld_pf:
        copy.wait()
    for l in range(2):
        stage[l, pl.ds(8, POS), :] = pf[l].astype(F32)
    for h in range(SLAB):
        for l in range(2):
            zfh[pl.ds(h * PLANE, PLANE), l * 128 : l * 128 + 128] = stage[
                l, pl.ds(8 + h, PLANE, stride=SLAB), :
            ].astype(BF16)
    for l in range(2):
        stage[l, pl.ds(0, 8), :] = jnp.zeros((8, 128), F32)
        stage[l, pl.ds(8 + POS, 8), :] = jnp.zeros((8, 128), F32)
        for side in range(2):
            hstage[side, l, pl.ds(0, 8), :] = jnp.zeros((8, 128), F32)
            hstage[side, l, pl.ds(8 + PLANE, 8), :] = jnp.zeros((8, 128), F32)

    for copy in ld_wd + ld_bo + ld_pz + ld_wl + ld_wc:
        copy.wait()

    acc[...] = jnp.zeros_like(acc)

    def project(step, carry):
        group = lax.rem(my_group + jnp.where(step == 0, 0, jnp.where(step == 1, 2, jnp.where(step == 2, 3, 1))), 4)
        for q in range(4):
            sender = group * 4 + q

            @pl.when(sender != me)
            def _():
                exchange(sender, sender).wait_recv()

        rows = pl.ds(pl.multiple_of(group * PLANE, PLANE), PLANE)
        for c in range(4):
            up = lax.dot_general(
                recv[rows, :], wd[pl.ds(c * 256, 256), :], NT, preferred_element_type=F32
            )
            for l in range(2):
                j = 2 * c + l
                at = slice(j * 128, j * 128 + 128)
                g = up[:, l * 128 : l * 128 + 128].astype(BF16).astype(F32)
                g = jnp.where(bo[j, rows, :].astype(F32) > 0, g, 0.0)
                glast[rows, at] = g.astype(BF16)
                z = pz[j, rows, :].astype(F32) - mean(2 * MID + 128 * j, 128)
                acc[0, :, at] += folded(g)
                acc[1, :, at] += folded(g * z)
        return carry

    lax.fori_loop(0, 4, project, 0)

    def share(slots, own, sends, recvs, axis):
        at = me if axis == "space" else dp

        def desc(other, sender):
            return pltpu.make_async_remote_copy(
                src_ref=slots.at[at],
                dst_ref=slots.at[sender],
                send_sem=sends.at[other],
                recv_sem=recvs.at[sender],
                device_id=(other, dp) if axis == "space" else (me, other),
                device_id_type=MESH,
            )

        slots[at] = own

        def go(k, carry):
            desc(lax.rem(at + k, 16), at).start()
            return carry

        lax.fori_loop(1, 16, go, 0)

        def finish():
            def wait(k, carry):
                other = lax.rem(at + k, 16)
                desc(other, other).wait_recv()
                return carry

            lax.fori_loop(1, 16, wait, 0)
            return jnp.sum(slots[...], axis=0)

        def drain():
            def wait(k, carry):
                desc(lax.rem(at + k, 16), at).wait_send()
                return carry

            lax.fori_loop(1, 16, wait, 0)

        return finish, drain

    def coefficients(sums, lo, n):
        scale = gain(lo, n) * rstd(lo, n)
        crossed = sums[1:2] * rstd(lo, n)
        slope = -scale * rstd(lo, n) * crossed * (1.0 / M)
        shift = -scale * sums[0:1] * (1.0 / M)
        return scale, slope, shift, crossed

    own = jnp.concatenate(
        [jnp.sum(acc[0], axis=0, keepdims=True), jnp.sum(acc[1], axis=0, keepdims=True)], axis=0
    )
    finish1, drain1 = share(st1, own, s1s, s1r, "space")
    sums1 = finish1()
    scale1, slope1, shift1, crossed1 = coefficients(sums1, 2 * MID, CH)
    std[dp, 0:1, 2 * MID :] = crossed1
    std[dp, 1:2, 2 * MID :] = sums1[0:1]

    acc[...] = jnp.zeros_like(acc)
    mean1 = mean(2 * MID, CH)

    def middle(step, carry):
        rows = pl.ds(pl.multiple_of(step * PLANE, PLANE), PLANE)
        for j in range(8):
            at = slice(j * 128, j * 128 + 128)
            z = pz[j, rows, :].astype(F32) - mean1[:, at]
            ldz[rows, at] = (
                glast[rows, at].astype(F32) * scale1[:, at] + z * slope1[:, at] + shift1[:, at]
            ).astype(BF16)
        mi = lax.dot_general(ldz[rows, :], wl[...], NT, preferred_element_type=F32)
        for l in range(2):
            at = slice(l * 128, l * 128 + 128)
            g = jnp.where(rm[l, rows, :].astype(F32) > 0, mi[:, at], 0.0)
            gmid[l, rows, :] = g
            acc[0, :, at] += folded(g)
            acc[1, :, at] += folded(g * zcm[l, rows, :])
        return carry

    lax.fori_loop(0, 4, middle, 0)
    own = jnp.concatenate(
        [
            jnp.sum(acc[0, :, :MID], axis=0, keepdims=True),
            jnp.sum(acc[1, :, :MID], axis=0, keepdims=True),
        ],
        axis=0,
    )
    finish2, drain2 = share(st2, own, s2s, s2r, "space")
    for slot, h in ((0, 0), (1, SLAB - 1)):
        for l in range(2):
            gsend[slot, :, l * 128 : l * 128 + 128] = gmid[
                l, pl.ds(h, PLANE, stride=SLAB), :
            ].astype(BF16)
    send_halos(gsend, ghalo, 1)

    def last(step, carry):
        cols = pl.ds(pl.multiple_of(step * 256, 256), 256)
        res = jnp.dot(rmt[...], ldz[:, cols], preferred_element_type=F32)
        pflat[0, pl.ds(step, MID, stride=4), :] = res[:, :128]
        pflat[1, pl.ds(step, MID, stride=4), :] = res[:, 128:]
        return carry

    lax.fori_loop(0, 4, last, 0)
    part[pl.ds(9 * MID, CH), :] = lanes(pflat, slice(None)).astype(BF16)

    core = lax.rem(me, 2)
    chip = lax.div(me, 2)
    partner = me + 1 - 2 * core

    def block(q, c):
        return pl.ds(pl.multiple_of((2 * q + c) * SHARE, SHARE), SHARE)

    def pair(q):
        return pltpu.make_async_remote_copy(
            src_ref=part.at[block(q, 1 - core)],
            dst_ref=ra.at[q],
            send_sem=as_.at[q],
            recv_sem=ar_.at[q],
            device_id=(partner, dp),
            device_id_type=MESH,
        )

    def chips(target, sender):
        return pltpu.make_async_remote_copy(
            src_ref=sb.at[target],
            dst_ref=rb.at[sender],
            send_sem=bs_.at[target],
            recv_sem=br_.at[sender],
            device_id=(2 * target + core, dp),
            device_id_type=MESH,
        )

    def start_pairs(lo, hi):
        def go(q, carry):
            pair(q).start()
            return carry

        lax.fori_loop(lo, hi, go, 0)

    def start_chips(lo, hi):
        def go(q, carry):
            pair(q).wait_recv()
            sb[q] = (part[block(q, core), :].astype(F32) + ra[q].astype(F32)).astype(BF16)

            @pl.when(q != chip)
            def _():
                chips(q, chip).start()

            return carry

        lax.fori_loop(lo, hi, go, 0)

    start_pairs(6, 8)

    sums2 = finish2()
    scale2, slope2, shift2, crossed2 = coefficients(sums2, MID, MID)
    std[dp, 0:1, MID : 2 * MID] = crossed2
    std[dp, 1:2, MID : 2 * MID] = sums2[0:1]

    for l in range(2):
        at = slice(l * 128, l * 128 + 128)
        stage[l, pl.ds(8, POS), :] = (
            (gmid[l] * scale2[:, at] + zcm[l] * slope2[:, at] + shift2[:, at])
            .astype(BF16)
            .astype(F32)
        )
    for h in range(SLAB):
        for l in range(2):
            for b in (-1, 0, 1):
                x = stage[l, pl.ds(8 + h - SLAB * b, PLANE, stride=SLAB), :]
                if b:
                    x = x * masks[(b + 1) // 2]
                lane = (b + 1) * MID + l * 128
                buf[pl.ds((h + 1) * PLANE, PLANE), lane : lane + 128] = x.astype(BF16)

    wait_halos(zsend, zhalo, 0)
    wait_halos(gsend, ghalo, 1)
    for side in range(2):
        present = me > 0 if side == 0 else me < NS - 1
        for l in range(2):
            at = slice(l * 128, l * 128 + 128)
            z = zhalo[side, :, at].astype(F32) - mean(MID + 128 * l, 128)
            dz = (
                (ghalo[side, :, at].astype(F32) * scale2[:, at] + z * slope2[:, at] + shift2[:, at])
                .astype(BF16)
                .astype(F32)
            )
            hstage[side, l, pl.ds(8, PLANE), :] = jnp.where(present, dz, 0.0)
            for b in (-1, 0, 1):
                x = hstage[side, l, pl.ds(8 - b, PLANE), :]
                if b:
                    x = x * masks[(b + 1) // 2]
                lane = (b + 1) * MID + l * 128
                buf[pl.ds(side * 5 * PLANE, PLANE), lane : lane + 128] = x.astype(BF16)

    def taps(step, carry):
        rows = pl.ds(pl.multiple_of((2 - step) * PLANE, PLANE), POS)
        for b in range(3):
            res = jnp.dot(
                rft[...], buf[rows, b * MID : b * MID + MID], preferred_element_type=F32
            )
            at = pl.ds(pl.multiple_of((3 * step + b) * MID, MID), MID)
            part[at, :] = res.astype(BF16)
        return carry

    lax.fori_loop(0, 3, taps, 0)
    start_pairs(0, 6)

    acc[...] = jnp.zeros_like(acc)
    mean3 = mean(0, MID)

    def conv(h, carry):
        total = jnp.zeros((PLANE, MID), F32)
        for a in range(3):
            rows = pl.ds(pl.multiple_of((h + 2 - a) * PLANE, PLANE), PLANE)
            total += lax.dot_general(buf[rows, :], wcat[a], NT, preferred_element_type=F32)
        rows = pl.ds(pl.multiple_of(h * PLANE, PLANE), PLANE)
        for l in range(2):
            at = slice(l * 128, l * 128 + 128)
            g = jnp.where(rfh[rows, at].astype(F32) > 0, total[:, at], 0.0)
            gfirst[l, pl.ds(h, PLANE, stride=SLAB), :] = g
            z = zfh[rows, at].astype(F32) - mean3[:, at]
            acc[0, :, at] += folded(g)
            acc[1, :, at] += folded(g * z)
        return carry

    lax.fori_loop(0, SLAB, conv, 0)
    own = jnp.concatenate(
        [
            jnp.sum(acc[0, :, :MID], axis=0, keepdims=True),
            jnp.sum(acc[1, :, :MID], axis=0, keepdims=True),
        ],
        axis=0,
    )
    finish3, drain3 = share(st3, own, s3s, s3r, "space")

    start_chips(0, 8)

    sums3 = finish3()
    scale3, slope3, shift3, crossed3 = coefficients(sums3, 0, MID)
    std[dp, 0:1, :MID] = crossed3
    std[dp, 1:2, :MID] = sums3[0:1]
    finish4, drain4 = share(std, std[dp], sds, sdr, "dp")

    for l in range(2):
        at = slice(l * 128, l * 128 + 128)
        z = pf[l].astype(F32) - mean3[:, at]
        ob[l] = (gfirst[l] * scale3[:, at] + z * slope3[:, at] + shift3[:, at]).astype(BF16)
    outs = [
        pltpu.make_async_copy(ob4.at[l], out_hbm.at[:, :, pl.ds(l * 128, 128)], osem.at[l])
        for l in range(2)
    ]
    for copy in outs:
        copy.start()

    tc[pl.ds(0, SHARE), :] = part[block(chip, core), :].astype(F32) + ra[chip].astype(F32)

    def gather(k, carry):
        sender = lax.rem(chip + k, 8)
        chips(sender, sender).wait_recv()
        tc[pl.ds(0, SHARE), :] += rb[sender].astype(F32)
        return carry

    lax.fori_loop(1, 8, gather, 0)
    tc[pl.ds(SHARE, 8), :] = jnp.zeros((8, 256), F32)
    for d in range(ND):
        sc[d] = tc[pl.ds(d * PIECE, 16), :].astype(BF16)
    rc[dp] = sc[dp]

    def shares(target, sender):
        return pltpu.make_async_remote_copy(
            src_ref=sc.at[target],
            dst_ref=rc.at[sender],
            send_sem=cs_.at[target],
            recv_sem=cr_.at[sender],
            device_id=(me, target),
            device_id_type=MESH,
        )

    def go(k, carry):
        shares(lax.rem(dp + k, ND), dp).start()
        return carry

    lax.fori_loop(1, ND, go, 0)

    ng_ref[...] = finish4() * FACTOR

    def wait(k, carry):
        other = lax.rem(dp + k, ND)
        shares(other, other).wait_recv()
        return carry

    lax.fori_loop(1, ND, wait, 0)
    mine = jnp.sum(rc[...].astype(F32), axis=0) * FACTOR
    for r in range(PIECE):
        wg_ref[2 * r : 2 * r + 1, :] = mine[r : r + 1, :128]
        wg_ref[2 * r + 1 : 2 * r + 2, :] = mine[r : r + 1, 128:]

    def drain_exchange(k, carry):
        exchange(lax.rem(me + k, NS), me).wait_send()
        return carry

    lax.fori_loop(1, NS, drain_exchange, 0)
    for drain in (drain1, drain2, drain3, drain4):
        drain()

    def drain_pairs(q, carry):
        pair(q).wait_send()

        @pl.when(q != chip)
        def _():
            chips(q, chip).wait_send()

        return carry

    lax.fori_loop(0, 8, drain_pairs, 0)

    def drain_shares(k, carry):
        shares(lax.rem(dp + k, ND), dp).wait_send()
        return carry

    lax.fori_loop(1, ND, drain_shares, 0)
    for copy in outs:
        copy.wait()


def shards(
    deep_grad, deep_weight, pre_first, relu_first, pre_middle, relu_middle, pre_last,
    block_output, weight_middle, weight_last, norm_mean, norm_rstd, norm_gain,
):
    def turned(x):
        return jnp.transpose(x, (0, 2, 1, 3)).reshape(PLANE, SLAB, x.shape[-1])

    any_spec = pl.BlockSpec(memory_space=pl.ANY)
    vmem_spec = pl.BlockSpec(memory_space=pltpu.VMEM)
    v = lambda shape, dtype: pltpu.VMEM(shape, dtype)
    dma = lambda *shape: pltpu.SemaphoreType.DMA(shape)
    scratch = [
        v((COLS, ROWS, MID4), BF16),
        v((NS, BLOCK, MID4), BF16),
        v((POS, MID4), BF16),
        v((CH, MID4), BF16),
        v((8, PLANE, SLAB, 128), BF16),
        v((8, PLANE, SLAB, 128), BF16),
        v((2, PLANE, SLAB, 128), BF16),
        v((2, PLANE, SLAB, 128), BF16),
        v((2, PLANE, SLAB, 128), BF16),
        v((2, PLANE, SLAB, 128), BF16),
        v((MID, CH), BF16),
        v((3, MID, 3 * MID), BF16),
        v((POS, CH), BF16),
        v((POS, CH), BF16),
        v((2, POS, 128), F32),
        v((2, POS, 128), F32),
        v((2, POS + 16, 128), F32),
        v((2, 2, PLANE + 16, 128), F32),
        v((6 * PLANE, 3 * MID), BF16),
        v((POS, MID), BF16),
        v((MID, POS), BF16),
        v((MID, POS), BF16),
        v((POS, MID), BF16),
        v((2, POS, 128), F32),
        v((2, PLANE, SLAB, 128), BF16),
        v((2, 8, CH), F32),
        v((NS, 2, CH), F32),
        v((NS, 2, MID), F32),
        v((NS, 2, MID), F32),
        v((ND, 2, CH + 2 * MID), F32),
        v((2, PLANE, MID), BF16),
        v((2, PLANE, MID), BF16),
        v((2, PLANE, MID), BF16),
        v((2, PLANE, MID), BF16),
        v((2, PLANE, 128), F32),
        v((2, CH, 128), F32),
        v((FLAT, 256), BF16),
        v((8, SHARE, 256), BF16),
        v((8, SHARE, 256), BF16),
        v((8, SHARE, 256), BF16),
        v((SHARE + 8, 256), F32),
        v((ND, 16, 256), BF16),
        v((ND, 16, 256), BF16),
        dma(36), dma(4), dma(2),
        dma(16), dma(16),
        dma(16), dma(16), dma(16), dma(16), dma(16), dma(16), dma(16), dma(16),
        dma(2, 2), dma(2, 2),
        dma(8), dma(8), dma(8), dma(8), dma(16), dma(16),
    ]
    first, weights, norms = pl.pallas_call(
        kernel,
        out_shape=(
            jax.ShapeDtypeStruct((PLANE, SLAB, MID), BF16),
            jax.ShapeDtypeStruct((2 * PIECE, 128), F32),
            jax.ShapeDtypeStruct((2, CH + 2 * MID), F32),
        ),
        in_specs=[any_spec] * 10 + [vmem_spec] * 3,
        out_specs=(any_spec, vmem_spec, vmem_spec),
        scratch_shapes=scratch,
        compiler_params=pltpu.CompilerParams(
            collective_id=0, has_side_effects=True, vmem_limit_bytes=60 << 20
        ),
    )(
        jnp.transpose(deep_grad, (0, 2, 1, 3)).reshape(COLS, ROWS, MID4),
        deep_weight,
        turned(pre_first),
        turned(relu_first),
        turned(pre_middle),
        turned(relu_middle),
        turned(pre_last),
        turned(block_output),
        weight_middle,
        weight_last,
        norm_mean,
        norm_rstd,
        norm_gain,
    )
    first = jnp.transpose(first.reshape(GROUP, COLS, SLAB, MID), (0, 2, 1, 3))
    return first, weights.reshape(-1), norms


def solution(mesh):
    return jax.shard_map(
        shards,
        mesh=mesh,
        in_specs=(
            P(("dp", "space"), None, None, None),
            P(),
            P("dp", "space", None, None),
            P("dp", "space", None, None),
            P("dp", "space", None, None),
            P("dp", "space", None, None),
            P("dp", "space", None, None),
            P("dp", "space", None, None),
            P(),
            P(),
            P(),
            P(),
            P(),
        ),
        out_specs=(P("dp", "space", None, None), P(("space", "dp")), P()),
        check_vma=False,
    )
```

time: 491 us -> 82.1 us (0.17)
  waiting for transfers between devices: 163 us -> 0 us
  blocking collectives: 157 us -> 0 us
  local copies, waits for them, and re-layouts: 82.7 us -> 4.78 us
  Pallas kernels: 0 us -> 75.3 us
  matrix products: 34.2 us -> 0 us
  other arithmetic: 22.6 us -> 0 us
  between operations: 14.7 us -> 0.64 us
  starting transfers between devices: 11.7 us -> 0 us
    psum x4 -> x0, blocking collectives: 157 us -> none  [the longest x3 91.4 us: norm_back(): group_totals, group_crossed = lax.psum((totals, crossed), 'space')]
    unnamed x2 -> x0, waiting for transfers between devices: 155 us -> none
    pallas_call x0 -> x1, Pallas kernels: none -> 75.3 us  [shards(): pl.pallas_call(kernel, out_shape=(jax.ShapeDtypeStruct((PLANE, SLAB, MID)...]
    dot_general x5 -> x0, matrix products: 34.2 us -> none  [the longest x1 12 us: shards(): jnp.dot(middle_flat.T, last_dz, preferred_element_type=jnp.float32)]
    convert_element_type x7 -> x0, local copies, waits for them, and re-layouts: 25.1 us -> none  [the longest x6 22.3 us: norm_back(): normed = (saved.astype(jnp.float32) - centre) * spread]
    unnamed x71 -> x3, local copies, waits for them, and re-layouts: 20.4 us -> 4.78 us
    concatenate x10 -> x0, local copies, waits for them, and re-layouts: 14.8 us -> none  [tap_columns(): stacked = jnp.concatenate(pieces, axis=-1)]
    gt x6 -> x0, local copies, waits for them, and re-layouts: 9.76 us -> none  [the longest x2 7.6 us: shards(): block_output.reshape(-1, channels) > 0]
  transfers between devices with their start and end apart: 4 -> 0, of which waited for: 2 -> 0; matrix products, arithmetic and copies ran while one was open for 13% -> 0% of each run, Pallas kernels for 0% -> 0%
where the time goes in v1:
time: 82.1 us; the launch traced here: 80.7 us
  Pallas kernels  75.3 us (92%)
  local copies, waits for them, and re-layouts  4.78 us (6%)
    pallas_call x1, Pallas kernels, shards(): pl.pallas_call(kernel, out_shape=(jax.ShapeDtypeStruct((PLANE, SLAB, MID)...  75.3 us
    unnamed x3, local copies, waits for them, and re-layouts  4.78 us

profile of v1, /device:TPU:1, one launch (start us, length us, event | category | flops | bytes accessed | tf_op | source)
XLA Modules:
  0.0 80.7 jit_solution(559241156047964264)
XLA Ops:
  0.6 75.3 %shard_map.148 = (bf16[320,4,256]{2,1,0:T(4,128)(2,1)}, f32[26,128]{1,0:T(8,128)}, f32[2,1536]{1,0:T(2,128)}) custom-call(bf16[20,64,512]{2,1,0:T(8,128)(2,1)} %bitcast.27, bf16[1024,512]{1,0:T(8,128)(2,1)} %wd_hbm.1, bf16[320,4,256]{2,1,0:T(4,128)(2,1)} %bitcast.28, bf16[320,4,256]{2,1,0:T(4,128)(2,1)} %bitcast.29, bf16[320,4,256]{2,1,0:T(4,128)(2,1)} %bitcast.30, ...), custom_call_target="tpu_custom_call" | custom-call | tf_op jit(solution)/shard_map/pallas_call | solution.py:656
  75.9 2.1 %copy.19 = bf16[16,4,20,256]{3,1,2,0:T(4,128)(2,1)} copy(bf16[16,4,20,256]{3,1,2,0:T(4,128)(2,1)} %bitcast.32) | data formatting | bytes 1310720
  78.1 1.3 %copy.20 = f32[3328]{0:T(1024)} copy(f32[3328]{0:T(1024)} %bitcast.33) | data formatting | bytes 26624
  79.4 1.3 %copy.21 = f32[2,1536]{1,0:T(2,128)} copy(f32[2,1536]{1,0:T(2,128)} %get-tuple-element.14) | data formatting | bytes 24576

commit v2 on v1

--- a/solution.py
+++ b/solution.py
@@ -30,6 +30,7 @@
 M = float(GROUP * ROWS * COLS)
 FACTOR = 1.0 / math.sqrt(M * ND)
 NT = (((1,), (1,)), ((), ()))
+ORDER = (12, 4, 13, 5, 11, 3, 10, 6, 14, 2, 9, 7, 15, 8, 1)
 
 
 def folded(values):
@@ -52,6 +53,7 @@
     lsem, dsem, osem,
     a2a_s, a2a_r, s1s, s1r, s2s, s2r, s3s, s3r, sds, sdr, hs, hr,
     as_, ar_, bs_, br_, cs_, cr_,
+    near, wide, other,
 ):
     me = lax.axis_index("space")
     dp = lax.axis_index("dp")
@@ -77,16 +79,21 @@
 
     barrier = pltpu.get_barrier_semaphore()
 
-    def greet(k, carry):
-        pl.semaphore_signal(
-            barrier, inc=1, device_id=(lax.rem(me + k, NS), dp), device_id_type=MESH
-        )
-        pl.semaphore_signal(
-            barrier, inc=1, device_id=(me, lax.rem(dp + k, ND)), device_id_type=MESH
-        )
-        return carry
-
-    lax.fori_loop(1, NS, greet, 0)
+    half, z = lax.div(dp, 8), lax.rem(dp, 8)
+
+    def along(k):
+        return (me, half * 8 + lax.rem(z + k, 8))
+
+    across = (me, lax.rem(dp + 8, ND))
+
+    def signal(sem, device):
+        pl.semaphore_signal(sem, inc=1, device_id=device, device_id_type=MESH)
+
+    for k in ORDER:
+        signal(barrier, (lax.rem(me + k, NS), dp))
+    signal(barrier, along(1))
+    signal(barrier, along(7))
+    signal(barrier, across)
 
     ld_pm = load_tiles(pm_hbm, pm4, 2)
     ld_rm = load_tiles(rm_hbm, rm4, 2)
@@ -119,36 +126,23 @@
             device_id_type=MESH,
         )
 
-    for copy in dg_copies:
-        copy.wait()
     my_group = lax.div(me, 4)
-
-    def pack(step, carry):
-        u = lax.rem(my_group + jnp.where(step == 0, 2, jnp.where(step == 1, 1, jnp.where(step == 2, 3, 0))), 4)
-        x = dgv[:, pl.ds(pl.multiple_of(u * 16, 16), 16), :].astype(F32)
-        low = lax.broadcasted_iota(jnp.int32, (10, 8, MID4), 1) < 4
-        for half in range(2):
-            y = x[:, 8 * half : 8 * half + 8, :].reshape(10, 2, 8, MID4)
+    low = lax.broadcasted_iota(jnp.int32, (10, 8, MID4), 1) < 4
+    for u in range(4):
+        dg_copies[u].wait()
+        x = dgv[:, 16 * u : 16 * u + 16, :].astype(F32)
+        for part_ in range(2):
+            y = x[:, 8 * part_ : 8 * part_ + 8, :].reshape(10, 2, 8, MID4)
             even, odd = y[:, 0], y[:, 1]
             first = jnp.where(low, even, pltpu.roll(odd, 4, 1))
             second = jnp.where(low, pltpu.roll(even, 4, 1), odd)
-            send[u * 4 + 2 * half] = first.reshape(BLOCK, MID4).astype(BF16)
-            send[u * 4 + 2 * half + 1] = second.reshape(BLOCK, MID4).astype(BF16)
-
-        @pl.when(step == 0)
-        def _():
-            pl.semaphore_wait(barrier, NS + ND - 2)
-
-        for q in range(4):
-            target = u * 4 + q
-
-            @pl.when(target != me)
-            def _():
-                exchange(target, me).start()
-
-        return carry
-
-    lax.fori_loop(0, 4, pack, 0)
+            send[u * 4 + 2 * part_] = first.reshape(BLOCK, MID4).astype(BF16)
+            send[u * 4 + 2 * part_ + 1] = second.reshape(BLOCK, MID4).astype(BF16)
+    pl.semaphore_wait(barrier, NS + 2)
+    for k in ORDER:
+        exchange(lax.rem(me + k, NS), me).start()
+    signal(near, along(1))
+    signal(near, along(7))
     recv[pl.ds(pl.multiple_of(me * BLOCK, BLOCK), BLOCK), :] = send[me]
 
     mean = lambda lo, n: mean_ref[pl.ds(lo, n)].reshape(1, n)
@@ -198,7 +192,6 @@
             zsend[slot, :, l * 128 : l * 128 + 128] = stage[
                 l, pl.ds(8 + h, PLANE, stride=SLAB), :
             ].astype(BF16)
-    send_halos(zsend, zhalo, 0)
 
     for copy in ld_rm:
         copy.wait()
@@ -240,6 +233,9 @@
 
     for copy in ld_wd + ld_bo + ld_pz + ld_wl + ld_wc:
         copy.wait()
+    pl.semaphore_wait(near, 2)
+    signal(wide, along(2))
+    signal(wide, along(6))
 
     acc[...] = jnp.zeros_like(acc)
 
@@ -285,11 +281,8 @@
 
         slots[at] = own
 
-        def go(k, carry):
+        for k in ORDER:
             desc(lax.rem(at + k, 16), at).start()
-            return carry
-
-        lax.fori_loop(1, 16, go, 0)
 
         def finish():
             def wait(k, carry):
@@ -320,6 +313,15 @@
         [jnp.sum(acc[0], axis=0, keepdims=True), jnp.sum(acc[1], axis=0, keepdims=True)], axis=0
     )
     finish1, drain1 = share(st1, own, s1s, s1r, "space")
+    send_halos(zsend, zhalo, 0)
+    pl.semaphore_wait(wide, 2)
+    signal(other, across)
+
+    def drain_exchange(k, carry):
+        exchange(lax.rem(me + k, NS), me).wait_send()
+        return carry
+
+    lax.fori_loop(1, NS, drain_exchange, 0)
     sums1 = finish1()
     scale1, slope1, shift1, crossed1 = coefficients(sums1, 2 * MID, CH)
     std[dp, 0:1, 2 * MID :] = crossed1
@@ -329,7 +331,7 @@
     mean1 = mean(2 * MID, CH)
 
     def middle(step, carry):
-        rows = pl.ds(pl.multiple_of(step * PLANE, PLANE), PLANE)
+        rows = pl.ds(step * PLANE, PLANE)
         for j in range(8):
             at = slice(j * 128, j * 128 + 128)
             z = pz[j, rows, :].astype(F32) - mean1[:, at]
@@ -345,7 +347,8 @@
             acc[1, :, at] += folded(g * zcm[l, rows, :])
         return carry
 
-    lax.fori_loop(0, 4, middle, 0)
+    for step in range(4):
+        middle(step, 0)
     own = jnp.concatenate(
         [
             jnp.sum(acc[0, :, :MID], axis=0, keepdims=True),
@@ -360,15 +363,17 @@
                 l, pl.ds(h, PLANE, stride=SLAB), :
             ].astype(BF16)
     send_halos(gsend, ghalo, 1)
+    drain1()
 
     def last(step, carry):
-        cols = pl.ds(pl.multiple_of(step * 256, 256), 256)
+        cols = pl.ds(step * 256, 256)
         res = jnp.dot(rmt[...], ldz[:, cols], preferred_element_type=F32)
         pflat[0, pl.ds(step, MID, stride=4), :] = res[:, :128]
         pflat[1, pl.ds(step, MID, stride=4), :] = res[:, 128:]
         return carry
 
-    lax.fori_loop(0, 4, last, 0)
+    for step in range(4):
+        last(step, 0)
     part[pl.ds(9 * MID, CH), :] = lanes(pflat, slice(None)).astype(BF16)
 
     core = lax.rem(me, 2)
@@ -461,18 +466,24 @@
                 lane = (b + 1) * MID + l * 128
                 buf[pl.ds(side * 5 * PLANE, PLANE), lane : lane + 128] = x.astype(BF16)
 
-    def taps(step, carry):
-        rows = pl.ds(pl.multiple_of((2 - step) * PLANE, PLANE), POS)
+    drain2()
+    start_chips(6, 8)
+
+    def taps(a):
+        rows = pl.ds((2 - a) * PLANE, POS)
         for b in range(3):
-            res = jnp.dot(
+            part[pl.ds((3 * a + b) * MID, MID), :] = jnp.dot(
                 rft[...], buf[rows, b * MID : b * MID + MID], preferred_element_type=F32
-            )
-            at = pl.ds(pl.multiple_of((3 * step + b) * MID, MID), MID)
-            part[at, :] = res.astype(BF16)
-        return carry
-
-    lax.fori_loop(0, 3, taps, 0)
-    start_pairs(0, 6)
+            ).astype(BF16)
+
+    taps(0)
+    start_pairs(0, 1)
+    taps(1)
+    start_pairs(1, 3)
+    start_chips(0, 1)
+    taps(2)
+    start_pairs(3, 6)
+    start_chips(1, 3)
 
     acc[...] = jnp.zeros_like(acc)
     mean3 = mean(0, MID)
@@ -480,9 +491,9 @@
     def conv(h, carry):
         total = jnp.zeros((PLANE, MID), F32)
         for a in range(3):
-            rows = pl.ds(pl.multiple_of((h + 2 - a) * PLANE, PLANE), PLANE)
+            rows = pl.ds((h + 2 - a) * PLANE, PLANE)
             total += lax.dot_general(buf[rows, :], wcat[a], NT, preferred_element_type=F32)
-        rows = pl.ds(pl.multiple_of(h * PLANE, PLANE), PLANE)
+        rows = pl.ds(h * PLANE, PLANE)
         for l in range(2):
             at = slice(l * 128, l * 128 + 128)
             g = jnp.where(rfh[rows, at].astype(F32) > 0, total[:, at], 0.0)
@@ -492,7 +503,10 @@
             acc[1, :, at] += folded(g * z)
         return carry
 
-    lax.fori_loop(0, SLAB, conv, 0)
+    for h in range(SLAB):
+        conv(h, 0)
+        if h == 1:
+            start_chips(3, 6)
     own = jnp.concatenate(
         [
             jnp.sum(acc[0, :, :MID], axis=0, keepdims=True),
@@ -502,13 +516,13 @@
     )
     finish3, drain3 = share(st3, own, s3s, s3r, "space")
 
-    start_chips(0, 8)
-
     sums3 = finish3()
     scale3, slope3, shift3, crossed3 = coefficients(sums3, 0, MID)
     std[dp, 0:1, :MID] = crossed3
     std[dp, 1:2, :MID] = sums3[0:1]
+    pl.semaphore_wait(other, 1)
     finish4, drain4 = share(std, std[dp], sds, sdr, "dp")
+    drain3()
 
     for l in range(2):
         at = slice(l * 128, l * 128 + 128)
@@ -545,11 +559,19 @@
             device_id_type=MESH,
         )
 
-    def go(k, carry):
+    for k in ORDER:
         shares(lax.rem(dp + k, ND), dp).start()
-        return carry
-
-    lax.fori_loop(1, ND, go, 0)
+
+    def drain_pairs(q, carry):
+        pair(q).wait_send()
+
+        @pl.when(q != chip)
+        def _():
+            chips(q, chip).wait_send()
+
+        return carry
+
+    lax.fori_loop(0, 8, drain_pairs, 0)
 
     ng_ref[...] = finish4() * FACTOR
 
@@ -564,24 +586,7 @@
         wg_ref[2 * r : 2 * r + 1, :] = mine[r : r + 1, :128]
         wg_ref[2 * r + 1 : 2 * r + 2, :] = mine[r : r + 1, 128:]
 
-    def drain_exchange(k, carry):
-        exchange(lax.rem(me + k, NS), me).wait_send()
-        return carry
-
-    lax.fori_loop(1, NS, drain_exchange, 0)
-    for drain in (drain1, drain2, drain3, drain4):
-        drain()
-
-    def drain_pairs(q, carry):
-        pair(q).wait_send()
-
-        @pl.when(q != chip)
-        def _():
-            chips(q, chip).wait_send()
-
-        return carry
-
-    lax.fori_loop(0, 8, drain_pairs, 0)
+    drain4()
 
     def drain_shares(k, carry):
         shares(lax.rem(dp + k, ND), dp).wait_send()
@@ -589,6 +594,16 @@
 
     lax.fori_loop(1, ND, drain_shares, 0)
     for copy in outs:
+        copy.wait()
+
+
+def settle(a, b, c, x, y, z, sem):
+    copies = [
+        pltpu.make_async_copy(src, dst, sem.at[i]) for i, (src, dst) in enumerate(((a, x), (b, y), (c, z)))
+    ]
+    for copy in copies:
+        copy.start()
+    for copy in copies:
         copy.wait()
 
 
@@ -652,6 +667,7 @@
         dma(16), dma(16), dma(16), dma(16), dma(16), dma(16), dma(16), dma(16),
         dma(2, 2), dma(2, 2),
         dma(8), dma(8), dma(8), dma(8), dma(16), dma(16),
+        pltpu.SemaphoreType.REGULAR, pltpu.SemaphoreType.REGULAR, pltpu.SemaphoreType.REGULAR,
     ]
     first, weights, norms = pl.pallas_call(
         kernel,
@@ -681,6 +697,14 @@
         norm_rstd,
         norm_gain,
     )
+    first, weights, norms = pl.pallas_call(
+        settle,
+        out_shape=tuple(jax.ShapeDtypeStruct(x.shape, x.dtype) for x in (first, weights, norms)),
+        in_specs=[any_spec] * 3,
+        out_specs=(any_spec,) * 3,
+        scratch_shapes=[dma(3)],
+        compiler_params=pltpu.CompilerParams(vmem_limit_bytes=60 << 20),
+    )(first, weights, norms)
     first = jnp.transpose(first.reshape(GROUP, COLS, SLAB, MID), (0, 2, 1, 3))
     return first, weights.reshape(-1), norms
 

time: 82.1 us -> 97 us (1.18); the launches traced: 80.7 us -> 96.8 us
  Pallas kernels: 75.3 us -> 96 us
  local copies, waits for them, and re-layouts: 4.78 us -> 0 us
    pallas_call x0 -> x1, Pallas kernels: none -> 21.8 us  [shards(): pl.pallas_call(settle, out_shape=tuple((jax.ShapeDtypeStruct(x.shape, x.d...]
    unnamed x3 -> x0, local copies, waits for them, and re-layouts: 4.78 us -> none
    pallas_call x1, Pallas kernels: 75.3 us -> 74.2 us  [shards(): pl.pallas_call(kernel, out_shape=(jax.ShapeDtypeStruct((PLANE, SLAB, MID)...]
where the time goes in v2:
time: 97 us; the launch traced here: 96.8 us
  Pallas kernels  96 us (99%)
    pallas_call x1, Pallas kernels, shards(): pl.pallas_call(kernel, out_shape=(jax.ShapeDtypeStruct((PLANE, SLAB, MID)...  74.2 us
    pallas_call x1, Pallas kernels, shards(): pl.pallas_call(settle, out_shape=tuple((jax.ShapeDtypeStruct(x.shape, x.d...  21.8 us

profile of v2, /device:TPU:1, one launch (start us, length us, event | category | flops | bytes accessed | tf_op | source)
XLA Modules:
  0.0 96.8 jit_solution(11375233398971287074)
XLA Ops:
  0.6 74.2 %shard_map.148 = (bf16[320,4,256]{2,1,0:T(4,128)(2,1)}, f32[26,128]{1,0:T(8,128)}, f32[2,1536]{1,0:T(2,128)}) custom-call(bf16[20,64,512]{2,1,0:T(8,128)(2,1)} %bitcast.27, bf16[1024,512]{1,0:T(8,128)(2,1)} %wd_hbm.1, bf16[320,4,256]{2,1,0:T(4,128)(2,1)} %bitcast.28, bf16[320,4,256]{2,1,0:T(4,128)(2,1)} %bitcast.29, bf16[320,4,256]{2,1,0:T(4,128)(2,1)} %bitcast.30, ...), custom_call_target="tpu_custom_call" | custom-call | tf_op jit(solution)/shard_map/pallas_call | solution.py:672
  74.9 21.8 %shard_map.149 = (bf16[320,4,256]{2,1,0:T(4,128)(2,1)}, f32[26,128]{1,0:T(8,128)}, f32[2,1536]{1,0:T(2,128)}) custom-call(bf16[320,4,256]{2,1,0:T(4,128)(2,1)} %get-tuple-element.9.a, f32[26,128]{1,0:T(8,128)} %get-tuple-element.10.b, f32[2,1536]{1,0:T(2,128)} %get-tuple-element.11.c), custom_call_target="tpu_custom_call" | custom-call | tf_op jit(solution)/shard_map/pallas_call | solution.py:700

commit v3 on v2

--- a/solution.py
+++ b/solution.py
@@ -47,7 +47,7 @@
     out_hbm, wg_ref, ng_ref,
     dgv, send, recv, wd, bo4, pz4, pf4, rf4, pm4, rm4, wl, wcat,
     glast, ldz, zcm, gmid, stage, hstage, buf, rfh, rft, rmt, zfh, gfirst, ob4,
-    acc, st1, st2, st3, std,
+    acc, st1, st2, st3, st4, std,
     zsend, gsend, zhalo, ghalo, masks,
     pflat, part, ra, sb, rb, tc, sc, rc,
     lsem, dsem, osem,
@@ -256,12 +256,12 @@
             for l in range(2):
                 j = 2 * c + l
                 at = slice(j * 128, j * 128 + 128)
-                g = up[:, l * 128 : l * 128 + 128].astype(BF16).astype(F32)
-                g = jnp.where(bo[j, rows, :].astype(F32) > 0, g, 0.0)
-                glast[rows, at] = g.astype(BF16)
-                z = pz[j, rows, :].astype(F32) - mean(2 * MID + 128 * j, 128)
+                g = up[:, l * 128 : l * 128 + 128].astype(BF16)
+                g = jnp.where(bo[j, rows, :] > 0, g, jnp.zeros_like(g))
+                glast[rows, at] = g
+                g = g.astype(F32)
                 acc[0, :, at] += folded(g)
-                acc[1, :, at] += folded(g * z)
+                acc[1, :, at] += folded(g * pz[j, rows, :].astype(F32))
         return carry
 
     lax.fori_loop(0, 4, project, 0)
@@ -309,9 +309,14 @@
         shift = -scale * sums[0:1] * (1.0 / M)
         return scale, slope, shift, crossed
 
-    own = jnp.concatenate(
-        [jnp.sum(acc[0], axis=0, keepdims=True), jnp.sum(acc[1], axis=0, keepdims=True)], axis=0
-    )
+    mean1 = mean(2 * MID, CH)
+
+    def local_sums(n, centre):
+        total = jnp.sum(acc[0, :, :n], axis=0, keepdims=True)
+        product = jnp.sum(acc[1, :, :n], axis=0, keepdims=True)
+        return jnp.concatenate([total, product - centre * total], axis=0)
+
+    own = local_sums(CH, mean1)
     finish1, drain1 = share(st1, own, s1s, s1r, "space")
     send_halos(zsend, zhalo, 0)
     pl.semaphore_wait(wide, 2)
@@ -324,17 +329,15 @@
     lax.fori_loop(1, NS, drain_exchange, 0)
     sums1 = finish1()
     scale1, slope1, shift1, crossed1 = coefficients(sums1, 2 * MID, CH)
-    std[dp, 0:1, 2 * MID :] = crossed1
-    std[dp, 1:2, 2 * MID :] = sums1[0:1]
+    shift1 = shift1 - slope1 * mean1
 
     acc[...] = jnp.zeros_like(acc)
-    mean1 = mean(2 * MID, CH)
 
     def middle(step, carry):
         rows = pl.ds(step * PLANE, PLANE)
         for j in range(8):
             at = slice(j * 128, j * 128 + 128)
-            z = pz[j, rows, :].astype(F32) - mean1[:, at]
+            z = pz[j, rows, :].astype(F32)
             ldz[rows, at] = (
                 glast[rows, at].astype(F32) * scale1[:, at] + z * slope1[:, at] + shift1[:, at]
             ).astype(BF16)
@@ -349,13 +352,7 @@
 
     for step in range(4):
         middle(step, 0)
-    own = jnp.concatenate(
-        [
-            jnp.sum(acc[0, :, :MID], axis=0, keepdims=True),
-            jnp.sum(acc[1, :, :MID], axis=0, keepdims=True),
-        ],
-        axis=0,
-    )
+    own = local_sums(MID, 0.0)
     finish2, drain2 = share(st2, own, s2s, s2r, "space")
     for slot, h in ((0, 0), (1, SLAB - 1)):
         for l in range(2):
@@ -363,6 +360,9 @@
                 l, pl.ds(h, PLANE, stride=SLAB), :
             ].astype(BF16)
     send_halos(gsend, ghalo, 1)
+    pl.semaphore_wait(other, 1)
+    own = jnp.concatenate([crossed1, sums1[0:1]], axis=0)
+    finish_last, drain_last = share(std, own, sds.at[0], sdr.at[0], "dp")
     drain1()
 
     def last(step, carry):
@@ -427,8 +427,6 @@
 
     sums2 = finish2()
     scale2, slope2, shift2, crossed2 = coefficients(sums2, MID, MID)
-    std[dp, 0:1, MID : 2 * MID] = crossed2
-    std[dp, 1:2, MID : 2 * MID] = sums2[0:1]
 
     for l in range(2):
         at = slice(l * 128, l * 128 + 128)
@@ -498,7 +496,7 @@
             at = slice(l * 128, l * 128 + 128)
             g = jnp.where(rfh[rows, at].astype(F32) > 0, total[:, at], 0.0)
             gfirst[l, pl.ds(h, PLANE, stride=SLAB), :] = g
-            z = zfh[rows, at].astype(F32) - mean3[:, at]
+            z = zfh[rows, at].astype(F32)
             acc[0, :, at] += folded(g)
             acc[1, :, at] += folded(g * z)
         return carry
@@ -507,27 +505,28 @@
         conv(h, 0)
         if h == 1:
             start_chips(3, 6)
+    own = local_sums(MID, mean3)
+    finish3, drain3 = share(st3, own, s3s, s3r, "space")
+    ng_ref[:, 2 * MID :] = finish_last() * FACTOR
+    drain_last()
+
+    sums3 = finish3()
+    scale3, slope3, shift3, crossed3 = coefficients(sums3, 0, MID)
     own = jnp.concatenate(
         [
-            jnp.sum(acc[0, :, :MID], axis=0, keepdims=True),
-            jnp.sum(acc[1, :, :MID], axis=0, keepdims=True),
+            jnp.concatenate([crossed3, crossed2], axis=1),
+            jnp.concatenate([sums3[0:1], sums2[0:1]], axis=1),
         ],
         axis=0,
     )
-    finish3, drain3 = share(st3, own, s3s, s3r, "space")
-
-    sums3 = finish3()
-    scale3, slope3, shift3, crossed3 = coefficients(sums3, 0, MID)
-    std[dp, 0:1, :MID] = crossed3
-    std[dp, 1:2, :MID] = sums3[0:1]
-    pl.semaphore_wait(other, 1)
-    finish4, drain4 = share(std, std[dp], sds, sdr, "dp")
+    finish4, drain4 = share(st4, own, sds.at[1], sdr.at[1], "dp")
     drain3()
 
     for l in range(2):
         at = slice(l * 128, l * 128 + 128)
-        z = pf[l].astype(F32) - mean3[:, at]
-        ob[l] = (gfirst[l] * scale3[:, at] + z * slope3[:, at] + shift3[:, at]).astype(BF16)
+        z = pf[l].astype(F32)
+        shift = shift3[:, at] - slope3[:, at] * mean3[:, at]
+        ob[l] = (gfirst[l] * scale3[:, at] + z * slope3[:, at] + shift).astype(BF16)
     outs = [
         pltpu.make_async_copy(ob4.at[l], out_hbm.at[:, :, pl.ds(l * 128, 128)], osem.at[l])
         for l in range(2)
@@ -573,7 +572,7 @@
 
     lax.fori_loop(0, 8, drain_pairs, 0)
 
-    ng_ref[...] = finish4() * FACTOR
+    ng_ref[:, : 2 * MID] = finish4() * FACTOR
 
     def wait(k, carry):
         other = lax.rem(dp + k, ND)
@@ -597,13 +596,16 @@
         copy.wait()
 
 
-def settle(a, b, c, x, y, z, sem):
-    copies = [
-        pltpu.make_async_copy(src, dst, sem.at[i]) for i, (src, dst) in enumerate(((a, x), (b, y), (c, z)))
-    ]
-    for copy in copies:
+def settle(a, b, c, x, y, z, va, vb, vc, sem):
+    arrays = ((a, va, x), (b, vb, y), (c, vc, z))
+    inward = [pltpu.make_async_copy(src, mid, sem.at[0, i]) for i, (src, mid, _) in enumerate(arrays)]
+    outward = [pltpu.make_async_copy(mid, dst, sem.at[1, i]) for i, (_, mid, dst) in enumerate(arrays)]
+    for copy in inward:
         copy.start()
-    for copy in copies:
+    for copy, onward in zip(inward, outward):
+        copy.wait()
+        onward.start()
+    for copy in outward:
         copy.wait()
 
 
@@ -648,7 +650,8 @@
         v((NS, 2, CH), F32),
         v((NS, 2, MID), F32),
         v((NS, 2, MID), F32),
-        v((ND, 2, CH + 2 * MID), F32),
+        v((ND, 2, 2 * MID), F32),
+        v((ND, 2, CH), F32),
         v((2, PLANE, MID), BF16),
         v((2, PLANE, MID), BF16),
         v((2, PLANE, MID), BF16),
@@ -664,7 +667,7 @@
         v((ND, 16, 256), BF16),
         dma(36), dma(4), dma(2),
         dma(16), dma(16),
-        dma(16), dma(16), dma(16), dma(16), dma(16), dma(16), dma(16), dma(16),
+        dma(16), dma(16), dma(16), dma(16), dma(16), dma(16), dma(2, 16), dma(2, 16),
         dma(2, 2), dma(2, 2),
         dma(8), dma(8), dma(8), dma(8), dma(16), dma(16),
         pltpu.SemaphoreType.REGULAR, pltpu.SemaphoreType.REGULAR, pltpu.SemaphoreType.REGULAR,
@@ -702,7 +705,7 @@
         out_shape=tuple(jax.ShapeDtypeStruct(x.shape, x.dtype) for x in (first, weights, norms)),
         in_specs=[any_spec] * 3,
         out_specs=(any_spec,) * 3,
-        scratch_shapes=[dma(3)],
+        scratch_shapes=[v(x.shape, x.dtype) for x in (first, weights, norms)] + [dma(2, 3)],
         compiler_params=pltpu.CompilerParams(vmem_limit_bytes=60 << 20),
     )(first, weights, norms)
     first = jnp.transpose(first.reshape(GROUP, COLS, SLAB, MID), (0, 2, 1, 3))

time: 97 us -> 75 us (0.77)
  Pallas kernels: 96 us -> 74 us
    pallas_call x1, Pallas kernels: 21.8 us -> 1.98 us  [shards(): pl.pallas_call(settle, out_shape=tuple((jax.ShapeDtypeStruct(x.shape, x.d...]
    pallas_call x1, Pallas kernels: 74.2 us -> 72.1 us  [shards(): pl.pallas_call(kernel, out_shape=(jax.ShapeDtypeStruct((PLANE, SLAB, MID)...]
where the time goes in v3:
time: 75 us; the launch traced here: 74.8 us
  Pallas kernels  74 us (99%)
  between operations  0.8 us (1%)
    pallas_call x1, Pallas kernels, shards(): pl.pallas_call(kernel, out_shape=(jax.ShapeDtypeStruct((PLANE, SLAB, MID)...  72.1 us
    pallas_call x1, Pallas kernels, shards(): pl.pallas_call(settle, out_shape=tuple((jax.ShapeDtypeStruct(x.shape, x.d...  1.98 us

profile of v3, /device:TPU:1, one launch (start us, length us, event | category | flops | bytes accessed | tf_op | source)
XLA Modules:
  0.0 74.8 jit_solution(14337436380607549156)
XLA Ops:
  0.6 72.1 %shard_map.148 = (bf16[320,4,256]{2,1,0:T(4,128)(2,1)}, f32[26,128]{1,0:T(8,128)}, f32[2,1536]{1,0:T(2,128)}) custom-call(bf16[20,64,512]{2,1,0:T(8,128)(2,1)} %bitcast.27, bf16[1024,512]{1,0:T(8,128)(2,1)} %wd_hbm.1, bf16[320,4,256]{2,1,0:T(4,128)(2,1)} %bitcast.28, bf16[320,4,256]{2,1,0:T(4,128)(2,1)} %bitcast.29, bf16[320,4,256]{2,1,0:T(4,128)(2,1)} %bitcast.30, ...), custom_call_target="tpu_custom_call" | custom-call | tf_op jit(solution)/shard_map/pallas_call | solution.py:675
  72.7 2.0 %shard_map.149 = (bf16[320,4,256]{2,1,0:T(4,128)(2,1)}, f32[26,128]{1,0:T(8,128)}, f32[2,1536]{1,0:T(2,128)}) custom-call(bf16[320,4,256]{2,1,0:T(4,128)(2,1)} %get-tuple-element.9.a, f32[26,128]{1,0:T(8,128)} %get-tuple-element.10.b, f32[2,1536]{1,0:T(2,128)} %get-tuple-element.11.c), custom_call_target="tpu_custom_call" | custom-call | tf_op jit(solution)/shard_map/pallas_call | solution.py:703

commit v4 on v3

--- a/solution.py
+++ b/solution.py
@@ -46,7 +46,7 @@
     mean_ref, rstd_ref, gain_ref,
     out_hbm, wg_ref, ng_ref,
     dgv, send, recv, wd, bo4, pz4, pf4, rf4, pm4, rm4, wl, wcat,
-    glast, ldz, zcm, gmid, stage, hstage, buf, rfh, rft, rmt, zfh, gfirst, ob4,
+    pzd, glast, ldz, zcm, gmid, stage, hstage, buf, rfh, rft, rmt, zfh, gfirst, ob4,
     acc, st1, st2, st3, st4, std,
     zsend, gsend, zhalo, ghalo, masks,
     pflat, part, ra, sb, rb, tc, sc, rc,
@@ -126,7 +126,6 @@
             device_id_type=MESH,
         )
 
-    my_group = lax.div(me, 4)
     low = lax.broadcasted_iota(jnp.int32, (10, 8, MID4), 1) < 4
     for u in range(4):
         dg_copies[u].wait()
@@ -233,14 +232,15 @@
 
     for copy in ld_wd + ld_bo + ld_pz + ld_wl + ld_wc:
         copy.wait()
+    for j in range(8):
+        pzd[:, j * 128 : j * 128 + 128] = pz[j]
     pl.semaphore_wait(near, 2)
     signal(wide, along(2))
     signal(wide, along(6))
 
     acc[...] = jnp.zeros_like(acc)
 
-    def project(step, carry):
-        group = lax.rem(my_group + jnp.where(step == 0, 0, jnp.where(step == 1, 2, jnp.where(step == 2, 3, 1))), 4)
+    def project(group):
         for q in range(4):
             sender = group * 4 + q
 
@@ -248,7 +248,7 @@
             def _():
                 exchange(sender, sender).wait_recv()
 
-        rows = pl.ds(pl.multiple_of(group * PLANE, PLANE), PLANE)
+        rows = pl.ds(group * PLANE, PLANE)
         for c in range(4):
             up = lax.dot_general(
                 recv[rows, :], wd[pl.ds(c * 256, 256), :], NT, preferred_element_type=F32
@@ -261,10 +261,10 @@
                 glast[rows, at] = g
                 g = g.astype(F32)
                 acc[0, :, at] += folded(g)
-                acc[1, :, at] += folded(g * pz[j, rows, :].astype(F32))
-        return carry
-
-    lax.fori_loop(0, 4, project, 0)
+                acc[1, :, at] += folded(g * pzd[rows, at].astype(F32))
+
+    for group in range(4):
+        project(group)
 
     def share(slots, own, sends, recvs, axis):
         at = me if axis == "space" else dp
@@ -335,13 +335,16 @@
 
     def middle(step, carry):
         rows = pl.ds(step * PLANE, PLANE)
+        tiles = []
         for j in range(8):
             at = slice(j * 128, j * 128 + 128)
-            z = pz[j, rows, :].astype(F32)
-            ldz[rows, at] = (
-                glast[rows, at].astype(F32) * scale1[:, at] + z * slope1[:, at] + shift1[:, at]
-            ).astype(BF16)
-        mi = lax.dot_general(ldz[rows, :], wl[...], NT, preferred_element_type=F32)
+            z = pzd[rows, at].astype(F32)
+            dz = glast[rows, at].astype(F32) * scale1[:, at] + z * slope1[:, at] + shift1[:, at]
+            tiles.append(dz.astype(BF16))
+            ldz[rows, at] = tiles[j]
+        mi = lax.dot_general(
+            jnp.concatenate(tiles, axis=1), wl[...], NT, preferred_element_type=F32
+        )
         for l in range(2):
             at = slice(l * 128, l * 128 + 128)
             g = jnp.where(rm[l, rows, :].astype(F32) > 0, mi[:, at], 0.0)
@@ -633,6 +636,7 @@
         v((2, PLANE, SLAB, 128), BF16),
         v((MID, CH), BF16),
         v((3, MID, 3 * MID), BF16),
+        v((POS, CH), BF16),
         v((POS, CH), BF16),
         v((POS, CH), BF16),
         v((2, POS, 128), F32),

time: 75 us -> 74.4 us (level)
  no operation moved by 1% of the time
where the time goes in v4:
time: 74.4 us; the launch traced here: 74.2 us
  Pallas kernels  73.4 us (99%)
  between operations  0.8 us (1%)
    pallas_call x1, Pallas kernels, shards(): pl.pallas_call(kernel, out_shape=(jax.ShapeDtypeStruct((PLANE, SLAB, MID)...  71.5 us
    pallas_call x1, Pallas kernels, shards(): pl.pallas_call(settle, out_shape=tuple((jax.ShapeDtypeStruct(x.shape, x.d...  1.98 us

profile of v4, /device:TPU:1, one launch (start us, length us, event | category | flops | bytes accessed | tf_op | source)
XLA Modules:
  0.0 74.2 jit_solution(10494560398322817972)
XLA Ops:
  0.6 71.5 %shard_map.148 = (bf16[320,4,256]{2,1,0:T(4,128)(2,1)}, f32[26,128]{1,0:T(8,128)}, f32[2,1536]{1,0:T(2,128)}) custom-call(bf16[20,64,512]{2,1,0:T(8,128)(2,1)} %bitcast.27, bf16[1024,512]{1,0:T(8,128)(2,1)} %wd_hbm.1, bf16[320,4,256]{2,1,0:T(4,128)(2,1)} %bitcast.28, bf16[320,4,256]{2,1,0:T(4,128)(2,1)} %bitcast.29, bf16[320,4,256]{2,1,0:T(4,128)(2,1)} %bitcast.30, ...), custom_call_target="tpu_custom_call" | custom-call | tf_op jit(solution)/shard_map/pallas_call | solution.py:679
  72.1 2.0 %shard_map.149 = (bf16[320,4,256]{2,1,0:T(4,128)(2,1)}, f32[26,128]{1,0:T(8,128)}, f32[2,1536]{1,0:T(2,128)}) custom-call(bf16[320,4,256]{2,1,0:T(4,128)(2,1)} %get-tuple-element.9.a, f32[26,128]{1,0:T(8,128)} %get-tuple-element.10.b, f32[2,1536]{1,0:T(2,128)} %get-tuple-element.11.c), custom_call_target="tpu_custom_call" | custom-call | tf_op jit(solution)/shard_map/pallas_call | solution.py:707

commit v5 on v4

--- a/solution.py
+++ b/solution.py
@@ -363,10 +363,7 @@
                 l, pl.ds(h, PLANE, stride=SLAB), :
             ].astype(BF16)
     send_halos(gsend, ghalo, 1)
-    pl.semaphore_wait(other, 1)
-    own = jnp.concatenate([crossed1, sums1[0:1]], axis=0)
-    finish_last, drain_last = share(std, own, sds.at[0], sdr.at[0], "dp")
-    drain1()
+    norm_last = jnp.concatenate([crossed1, sums1[0:1]], axis=0)
 
     def last(step, carry):
         cols = pl.ds(step * 256, 256)
@@ -427,7 +424,7 @@
         lax.fori_loop(lo, hi, go, 0)
 
     start_pairs(6, 8)
-
+    start_chips(6, 8)
     sums2 = finish2()
     scale2, slope2, shift2, crossed2 = coefficients(sums2, MID, MID)
 
@@ -467,8 +464,6 @@
                 lane = (b + 1) * MID + l * 128
                 buf[pl.ds(side * 5 * PLANE, PLANE), lane : lane + 128] = x.astype(BF16)
 
-    drain2()
-    start_chips(6, 8)
 
     def taps(a):
         rows = pl.ds((2 - a) * PLANE, POS)
@@ -506,12 +501,14 @@
 
     for h in range(SLAB):
         conv(h, 0)
-        if h == 1:
+        if h == 0:
             start_chips(3, 6)
     own = local_sums(MID, mean3)
     finish3, drain3 = share(st3, own, s3s, s3r, "space")
-    ng_ref[:, 2 * MID :] = finish_last() * FACTOR
-    drain_last()
+    pl.semaphore_wait(other, 1)
+    finish_last, drain_last = share(std, norm_last, sds.at[0], sdr.at[0], "dp")
+    drain1()
+    drain2()
 
     sums3 = finish3()
     scale3, slope3, shift3, crossed3 = coefficients(sums3, 0, MID)
@@ -575,11 +572,22 @@
 
     lax.fori_loop(0, 8, drain_pairs, 0)
 
+    ng_ref[:, 2 * MID :] = finish_last() * FACTOR
+    drain_last()
     ng_ref[:, : 2 * MID] = finish4() * FACTOR
+    drain4()
+
+    def drain_shares(k, carry):
+        shares(lax.rem(dp + k, ND), dp).wait_send()
+        return carry
+
+    lax.fori_loop(1, ND, drain_shares, 0)
+    for copy in outs:
+        copy.wait()
 
     def wait(k, carry):
-        other = lax.rem(dp + k, ND)
-        shares(other, other).wait_recv()
+        sender = lax.rem(dp + k, ND)
+        shares(sender, sender).wait_recv()
         return carry
 
     lax.fori_loop(1, ND, wait, 0)
@@ -587,16 +595,6 @@
     for r in range(PIECE):
         wg_ref[2 * r : 2 * r + 1, :] = mine[r : r + 1, :128]
         wg_ref[2 * r + 1 : 2 * r + 2, :] = mine[r : r + 1, 128:]
-
-    drain4()
-
-    def drain_shares(k, carry):
-        shares(lax.rem(dp + k, ND), dp).wait_send()
-        return carry
-
-    lax.fori_loop(1, ND, drain_shares, 0)
-    for copy in outs:
-        copy.wait()
 
 
 def settle(a, b, c, x, y, z, va, vb, vc, sem):

time: 74.4 us -> 73.6 us (0.989)
  Pallas kernels: 73.4 us -> 72.3 us
    pallas_call x1, Pallas kernels: 71.5 us -> 70.3 us  [shards(): pl.pallas_call(kernel, out_shape=(jax.ShapeDtypeStruct((PLANE, SLAB, MID)...]
where the time goes in v5:
time: 73.6 us; the launch traced here: 73.1 us
  Pallas kernels  72.3 us (98%)
  between operations  0.8 us (1%)
    pallas_call x1, Pallas kernels, shards(): pl.pallas_call(kernel, out_shape=(jax.ShapeDtypeStruct((PLANE, SLAB, MID)...  70.3 us
    pallas_call x1, Pallas kernels, shards(): pl.pallas_call(settle, out_shape=tuple((jax.ShapeDtypeStruct(x.shape, x.d...  1.98 us

profile of v5, /device:TPU:1, one launch (start us, length us, event | category | flops | bytes accessed | tf_op | source)
XLA Modules:
  0.0 73.1 jit_solution(11555217622261975077)
XLA Ops:
  0.6 70.3 %shard_map.148 = (bf16[320,4,256]{2,1,0:T(4,128)(2,1)}, f32[26,128]{1,0:T(8,128)}, f32[2,1536]{1,0:T(2,128)}) custom-call(bf16[20,64,512]{2,1,0:T(8,128)(2,1)} %bitcast.27, bf16[1024,512]{1,0:T(8,128)(2,1)} %wd_hbm.1, bf16[320,4,256]{2,1,0:T(4,128)(2,1)} %bitcast.28, bf16[320,4,256]{2,1,0:T(4,128)(2,1)} %bitcast.29, bf16[320,4,256]{2,1,0:T(4,128)(2,1)} %bitcast.30, ...), custom_call_target="tpu_custom_call" | custom-call | tf_op jit(solution)/shard_map/pallas_call | solution.py:677
  71.0 2.0 %shard_map.149 = (bf16[320,4,256]{2,1,0:T(4,128)(2,1)}, f32[26,128]{1,0:T(8,128)}, f32[2,1536]{1,0:T(2,128)}) custom-call(bf16[320,4,256]{2,1,0:T(4,128)(2,1)} %get-tuple-element.9.a, f32[26,128]{1,0:T(8,128)} %get-tuple-element.10.b, f32[2,1536]{1,0:T(2,128)} %get-tuple-element.11.c), custom_call_target="tpu_custom_call" | custom-call | tf_op jit(solution)/shard_map/pallas_call | solution.py:705

commit v6 on v5

--- a/solution.py
+++ b/solution.py
@@ -374,7 +374,7 @@
 
     for step in range(4):
         last(step, 0)
-    part[pl.ds(9 * MID, CH), :] = lanes(pflat, slice(None)).astype(BF16)
+    part[pl.ds(9 * MID, CH), :] = lanes(pflat, slice(0, CH)).astype(BF16)
 
     core = lax.rem(me, 2)
     chip = lax.div(me, 2)
@@ -431,7 +431,7 @@
     for l in range(2):
         at = slice(l * 128, l * 128 + 128)
         stage[l, pl.ds(8, POS), :] = (
-            (gmid[l] * scale2[:, at] + zcm[l] * slope2[:, at] + shift2[:, at])
+            (gmid[l, pl.ds(0, POS), :] * scale2[:, at] + zcm[l] * slope2[:, at] + shift2[:, at])
             .astype(BF16)
             .astype(F32)
         )
@@ -526,7 +526,7 @@
         at = slice(l * 128, l * 128 + 128)
         z = pf[l].astype(F32)
         shift = shift3[:, at] - slope3[:, at] * mean3[:, at]
-        ob[l] = (gfirst[l] * scale3[:, at] + z * slope3[:, at] + shift).astype(BF16)
+        ob[l] = (gfirst[l, pl.ds(0, POS), :] * scale3[:, at] + z * slope3[:, at] + shift).astype(BF16)
     outs = [
         pltpu.make_async_copy(ob4.at[l], out_hbm.at[:, :, pl.ds(l * 128, 128)], osem.at[l])
         for l in range(2)
@@ -638,7 +638,7 @@
         v((POS, CH), BF16),
         v((POS, CH), BF16),
         v((2, POS, 128), F32),
-        v((2, POS, 128), F32),
+        v((2, POS + 8, 128), F32),
         v((2, POS + 16, 128), F32),
         v((2, 2, PLANE + 16, 128), F32),
         v((6 * PLANE, 3 * MID), BF16),
@@ -646,7 +646,7 @@
         v((MID, POS), BF16),
         v((MID, POS), BF16),
         v((POS, MID), BF16),
-        v((2, POS, 128), F32),
+        v((2, POS + 8, 128), F32),
         v((2, PLANE, SLAB, 128), BF16),
         v((2, 8, CH), F32),
         v((NS, 2, CH), F32),
@@ -659,7 +659,7 @@
         v((2, PLANE, MID), BF16),
         v((2, PLANE, MID), BF16),
         v((2, PLANE, 128), F32),
-        v((2, CH, 128), F32),
+        v((2, CH + 8, 128), F32),
         v((FLAT, 256), BF16),
         v((8, SHARE, 256), BF16),
         v((8, SHARE, 256), BF16),

time: 73.6 us -> 73.5 us (level)
  no operation moved by 1% of the time
where the time goes in v6:
time: 73.5 us; the launch traced here: 73.1 us
  Pallas kernels  72.3 us (98%)
  between operations  0.8 us (1%)
    pallas_call x1, Pallas kernels, shards(): pl.pallas_call(kernel, out_shape=(jax.ShapeDtypeStruct((PLANE, SLAB, MID)...  70.4 us
    pallas_call x1, Pallas kernels, shards(): pl.pallas_call(settle, out_shape=tuple((jax.ShapeDtypeStruct(x.shape, x.d...  1.98 us

profile of v6, /device:TPU:1, one launch (start us, length us, event | category | flops | bytes accessed | tf_op | source)
XLA Modules:
  0.0 73.1 jit_solution(8351296496532631285)
XLA Ops:
  0.6 70.4 %shard_map.148 = (bf16[320,4,256]{2,1,0:T(4,128)(2,1)}, f32[26,128]{1,0:T(8,128)}, f32[2,1536]{1,0:T(2,128)}) custom-call(bf16[20,64,512]{2,1,0:T(8,128)(2,1)} %bitcast.27, bf16[1024,512]{1,0:T(8,128)(2,1)} %wd_hbm.1, bf16[320,4,256]{2,1,0:T(4,128)(2,1)} %bitcast.28, bf16[320,4,256]{2,1,0:T(4,128)(2,1)} %bitcast.29, bf16[320,4,256]{2,1,0:T(4,128)(2,1)} %bitcast.30, ...), custom_call_target="tpu_custom_call" | custom-call | tf_op jit(solution)/shard_map/pallas_call | solution.py:677
  71.0 2.0 %shard_map.149 = (bf16[320,4,256]{2,1,0:T(4,128)(2,1)}, f32[26,128]{1,0:T(8,128)}, f32[2,1536]{1,0:T(2,128)}) custom-call(bf16[320,4,256]{2,1,0:T(4,128)(2,1)} %get-tuple-element.9.a, f32[26,128]{1,0:T(8,128)} %get-tuple-element.10.b, f32[2,1536]{1,0:T(2,128)} %get-tuple-element.11.c), custom_call_target="tpu_custom_call" | custom-call | tf_op jit(solution)/shard_map/pallas_call | solution.py:705
